TPU v7x, 128 devices: a whole 4x4x4 slice. The times are simulated.
128 devices in a mesh: row: 16 (over y, x), samp: 8 (over z, core).
Axes of the slice: x: 4, y: 4, z: 4, core: 2. Of those that a mesh axis runs over, the one named last changes fastest.
Arguments:
- fibres_first: float32 [16384, 16384], P('row', 'samp'), may hold values from -768 to 768
- fibres_second: float32 [16384, 16384], P('row', 'samp'), may hold values from -768 to 768
- index_first: int32 [16384, 2], P('samp'), may hold values from 0 to 16383, as said below
- index_second: int32 [16384, 2], P('samp'), may hold values from 0 to 16383, as said below
- factor_b: float32 [16384, 256], P('row'), may hold values from -6 to 6
- factor_c: float32 [16384, 256], P('row'), may hold values from -6 to 6
Outputs:
- factor_a: float32 [16384, 256], P('row')
- factor_b_new: float32 [16384, 256], P('row')
- weights: float32 [256], replicated
Inputs may be any that keep to these rules, and one draw needn't show every extreme that they name: `index_first`: in each aligned block of 128 samples and in each column, at most 16 indices fall into the range of one block of 1024 factor rows; in every block some range takes exactly 16. `index_second`: in each aligned block of 128 samples and in each column, at most 16 indices fall into the range of one block of 1024 factor rows; in every block some range takes exactly 16.
All inputs are finite; a program needn't handle non-finite values.
Results may differ from a plain program's by a relative error of at most 0.00017.
Values sent between devices are 32-bit elements; how exact they have to be, the bound alone decides.
No kernel may reach another device: no remote copies, remote signals or barrier semaphores. Data moves between devices by JAX's collectives and lax.ppermute only.
A program may use at most 128 MiB of HBM per device.

v0:
```python
import jax
import jax.numpy as jnp
from jax import lax
from jax.sharding import PartitionSpec as P


def select_rows(owned, wanted):
    height = owned.shape[0]
    local_idx = wanted - lax.axis_index("row") * height
    inside = (local_idx >= 0) & (local_idx < height)
    picked = jnp.take(owned, jnp.clip(local_idx, 0, height - 1), axis=0)
    return jnp.where(inside[:, None], picked, jnp.zeros_like(picked))


def gram_of(khatri):
    return jnp.dot(khatri.T, khatri, precision=lax.Precision.HIGHEST)


def solve_mode(fibres, first_owned, second_owned, index_pairs):
    picked_first = select_rows(first_owned, index_pairs[:, 0])
    picked_second = select_rows(second_owned, index_pairs[:, 1])
    rows_first, rows_second = lax.psum((picked_first, picked_second), "row")
    khatri = rows_first * rows_second
    gram_matrix = lax.psum(gram_of(khatri), "samp")
    partial_product = jnp.dot(fibres, khatri, precision=lax.Precision.HIGHEST)
    lower_factor = jnp.linalg.cholesky(gram_matrix)
    total_rows = first_owned.shape[0] * lax.axis_size("row")
    product = lax.psum(partial_product, "samp")
    solved = jax.scipy.linalg.cho_solve((lower_factor, True), product.T).T
    squares_sum = lax.psum(jnp.sum(solved * solved, axis=0), "row")
    scales = jnp.sqrt(squares_sum / total_rows + 1e-06)
    return (solved / scales, scales)


def shards(fibres_first, fibres_second, index_first, index_second, factor_b, factor_c):
    factor_a, scale_first = solve_mode(fibres_first, factor_b, factor_c, index_first)
    factor_b_new, weights = solve_mode(fibres_second, factor_a, factor_c, index_second)
    return (factor_a, factor_b_new, weights)


def solution(mesh):
    placed = (
        P("row", "samp"),
        P("row", "samp"),
        P("samp", None),
        P("samp", None),
        P("row", None),
        P("row", None),
    )
    return jax.shard_map(
        shards,
        mesh=mesh,
        in_specs=placed,
        out_specs=(P("row", None), P("row", None), P()),
        check_vma=False,
    )
```

profile of v0, /device:TPU:0, one launch (start us, length us, event | category | flops | bytes accessed | tf_op | source)
XLA Modules:
  0.0 649.8 jit_solution(11864826749617288509)
XLA Ops:
  7.2 0.9 broadcast_clamp_fusion
  8.2 0.9 and_reduce_fusion
  9.1 8.6 %gather_fusion.1 = f32[2048,256]{1,0:T(8,128)} fusion(f32[1024,256]{1,0:T(8,128)S(1)} %copy-done, s32[2048]{0:T(1024)S(1)} %fusion.31), kind=kCustom, calls=%fused_computation.1.clone | custom fusion | bytes 4202496 | tf_op jit(solution)/shard_map/jit(_take)/gather | solution.py:11
  17.7 8.6 %gather_fusion = f32[2048,256]{1,0:T(8,128)} fusion(f32[1024,256]{1,0:T(8,128)S(1)} %copy-done.2, s32[2048]{0:T(1024)S(1)} %fusion.30), kind=kCustom, calls=%fused_computation.clone | custom fusion | bytes 4202496 | tf_op jit(solution)/shard_map/jit(_take)/gather | solution.py:11
  26.3 4.4 select_select_fusion.2
  30.7 2.7 select_select_fusion.3
  33.5 6.6 %gather_fusion.3 = f32[2048,256]{1,0:T(8,128)S(1)} fusion(f32[1024,256]{1,0:T(8,128)S(1)} %copy-done, s32[2048]{0:T(1024)S(1)} %fusion.33), kind=kCustom, calls=%fused_computation.3.clone | custom fusion | bytes 4202496 | tf_op jit(solution)/shard_map/jit(_take)/gather | solution.py:11
  40.2 99.4 %all-reduce.12.cloned.1.call-done = (f32[2048,256]{1,0:T(8,128)}, f32[2048,256]{1,0:T(8,128)}) async-done(((f32[2048,256]{1,0:T(8,128)}, f32[2048,256]{1,0:T(8,128)}), (f32[2048,256]{1,0:T(8,128)}, f32[2048,256]{1,0:T(8,128)})) %all-reduce.12.cloned.1.call-update) | async-done | bytes 4194320 | tf_op jit(solution)/shard_map/psum | solution.py:22
  139.6 7.8 %fusion.6 = f32[256,256]{0,1:T(8,128)} fusion(f32[2048,256]{1,0:T(8,128)} %get-tuple-element.47, f32[2048,256]{1,0:T(8,128)} %get-tuple-element.48), kind=kOutput, calls=%fused_computation.30 | convolution fusion | flops 1611137024 | bytes 4456448 | tf_op jit(solution)/shard_map/dot_general | solution.py:16
  147.4 16.9 %fusion.4 = f32[256,1024]{1,0:T(8,128)} fusion(f32[1024,2048]{1,0:T(8,128)} %param.11, f32[2048,256]{1,0:T(8,128)S(1)} %copy-done.4, f32[2048,256]{1,0:T(8,128)S(1)} %copy-done.5), kind=kOutput, calls=%fused_computation.28 | convolution fusion | flops 6442975232 | bytes 13631488 | tf_op jit(solution)/shard_map/dot_general | solution.py:25
  164.6 2.8 select_select_fusion
  167.3 60.6 %all-reduce.16.cloned.1.call-done = (f32[256,1024]{1,0:T(8,128)}, f32[256,256]{0,1:T(8,128)}) async-done(((f32[256,1024]{1,0:T(8,128)}, f32[256,256]{0,1:T(8,128)}), (f32[256,1024]{1,0:T(8,128)}, f32[256,256]{0,1:T(8,128)})) %all-reduce.16.cloned.1.call-update) | async-done | bytes 1310736 | tf_op jit(solution)/shard_map/psum | solution.py:28
  228.0 1.2 copy.10
  229.1 1.0 fusion.13
  230.1 11.7 %cholesky.130 = f32[128,128]{1,0:T(8,128)S(1)} custom-call(f32[128,128]{1,0:T(8,128)S(1)} %cholesky.194), custom_call_target="Cholesky" | custom-call | tf_op jit(solution)/shard_map/jit(cholesky)/cholesky | solution.py:26
  241.9 9.8 %custom-call.15 = f32[1,128,128]{1,2,0:T(8,128)S(1)} custom-call(f32[1,128,128]{2,1,0:T(8,128)S(1)} %get-tuple-element.64), custom_call_target="InvertDiagBlocksLowerTriangular" | custom-call | tf_op jit(solution)/shard_map/jit(cholesky)/cholesky | solution.py:26
  252.2 11.7 %cholesky.147 = f32[128,128]{1,0:T(8,128)S(1)} custom-call(f32[128,128]{1,0:T(8,128)S(1)} %convolution_subtract_fusion.5), custom_call_target="Cholesky" | custom-call | tf_op jit(solution)/shard_map/jit(cholesky)/cholesky | solution.py:26
  264.0 0.6 compare_reduce_fusion.2
  264.6 0.6 compare_reduce_fusion.3
  266.6 4.0 while.4
  267.3 1.4 bitcast_dynamic-update-slice_fusion.4
  269.3 1.4 bitcast_dynamic-update-slice_fusion.4
  270.7 20.1 %custom-call.16 = f32[2,128,128]{1,2,0:T(8,128)S(1)} custom-call(f32[2,128,128]{2,1,0:T(8,128)S(1)} %get-tuple-element.20), custom_call_target="InvertDiagBlocksLowerTriangular" | custom-call | tf_op jit(solution)/shard_map/jit(_cho_solve)/triangular_solve | solution.py:29
  290.8 0.6 fusion.10
  292.0 0.6 fusion.22
  293.2 0.6 convolution_subtract_fusion.2
  294.6 40.3 %psum.74 = f32[256]{0:T(256)S(1)} all-reduce(f32[256]{0:T(256)S(1)} %multiply_reduce_fusion.1), channel_id=1, replica_groups=mesh['row'=16,'samp'=8] {'row'}, use_global_device_ids=true, to_apply=%region_9.13 | all-reduce | flops 256 | bytes 2048 | tf_op jit(solution)/shard_map/psum | solution.py:30
  335.4 8.6 %gather_fusion.2 = f32[2048,256]{1,0:T(8,128)} fusion(f32[1024,256]{1,0:T(8,128)S(1)} %copy.14, s32[2048]{0:T(1024)S(1)} %fusion.32), kind=kCustom, calls=%fused_computation.2.clone | custom fusion | bytes 4202496 | tf_op jit(solution)/shard_map/jit(_take)/gather | solution.py:11
  344.0 4.3 select_select_fusion.1
  348.4 97.2 %all-reduce.10.cloned.1.call-done = (f32[2048,256]{1,0:T(8,128)}, f32[2048,256]{1,0:T(8,128)}) async-done(((f32[2048,256]{1,0:T(8,128)}, f32[2048,256]{1,0:T(8,128)}), (f32[2048,256]{1,0:T(8,128)}, f32[2048,256]{1,0:T(8,128)})) %all-reduce.10.cloned.1.call-update) | async-done | bytes 4194320 | tf_op jit(solution)/shard_map/psum | solution.py:22
  445.6 7.8 %fusion.2 = f32[256,256]{0,1:T(8,128)} fusion(f32[2048,256]{1,0:T(8,128)} %get-tuple-element.45, f32[2048,256]{1,0:T(8,128)} %get-tuple-element.46), kind=kOutput, calls=%fused_computation.26 | convolution fusion | flops 1611137024 | bytes 4456448 | tf_op jit(solution)/shard_map/dot_general | solution.py:16
  453.4 17.3 %fusion = f32[256,1024]{1,0:T(8,128)} fusion(f32[1024,2048]{1,0:T(8,128)} %param.12, f32[2048,256]{1,0:T(8,128)S(1)} %copy-done.6, f32[2048,256]{1,0:T(8,128)S(1)} %copy-done.7), kind=kOutput, calls=%fused_computation.24 | convolution fusion | flops 6442975232 | bytes 13631488 | tf_op jit(solution)/shard_map/dot_general | solution.py:25
  470.7 63.6 %all-reduce.14.cloned.1.call-done = (f32[256,1024]{1,0:T(8,128)}, f32[256,256]{0,1:T(8,128)}) async-done(((f32[256,1024]{1,0:T(8,128)}, f32[256,256]{0,1:T(8,128)}), (f32[256,1024]{1,0:T(8,128)}, f32[256,256]{0,1:T(8,128)})) %all-reduce.14.cloned.1.call-update) | async-done | bytes 1310736 | tf_op jit(solution)/shard_map/psum | solution.py:28
  534.4 1.2 copy.13
  535.5 1.0 fusion.12
  536.5 11.7 %cholesky.164 = f32[128,128]{1,0:T(8,128)S(1)} custom-call(f32[128,128]{1,0:T(8,128)S(1)} %cholesky.197), custom_call_target="Cholesky" | custom-call | tf_op jit(solution)/shard_map/jit(cholesky)/cholesky | solution.py:26
  548.3 9.8 %custom-call.17 = f32[1,128,128]{1,2,0:T(8,128)S(1)} custom-call(f32[1,128,128]{2,1,0:T(8,128)S(1)} %get-tuple-element.60), custom_call_target="InvertDiagBlocksLowerTriangular" | custom-call | tf_op jit(solution)/shard_map/jit(cholesky)/cholesky | solution.py:26
  558.6 11.7 %cholesky.181 = f32[128,128]{1,0:T(8,128)S(1)} custom-call(f32[128,128]{1,0:T(8,128)S(1)} %convolution_subtract_fusion.4), custom_call_target="Cholesky" | custom-call | tf_op jit(solution)/shard_map/jit(cholesky)/cholesky | solution.py:26
  570.4 0.7 compare_reduce_fusion
  571.1 0.6 compare_reduce_fusion.1
  573.1 4.1 while.5
  573.7 1.4 bitcast_dynamic-update-slice_fusion.5
  575.8 1.4 bitcast_dynamic-update-slice_fusion.5
  577.2 19.9 %custom-call.18 = f32[2,128,128]{1,2,0:T(8,128)S(1)} custom-call(f32[2,128,128]{2,1,0:T(8,128)S(1)} %get-tuple-element.21), custom_call_target="InvertDiagBlocksLowerTriangular" | custom-call | tf_op jit(solution)/shard_map/jit(_cho_solve)/triangular_solve | solution.py:29
  598.4 0.6 fusion.25
  599.6 0.6 convolution_subtract_fusion
  601.0 40.3 %psum.79 = f32[256]{0:T(256)S(1)} all-reduce(f32[256]{0:T(256)S(1)} %multiply_reduce_fusion), channel_id=1, replica_groups=mesh['row'=16,'samp'=8] {'row'}, use_global_device_ids=true, to_apply=%region_15.19 | all-reduce | flops 256 | bytes 2048 | tf_op jit(solution)/shard_map/psum | solution.py:30
  641.5 1.3 copy.15
  (78 shorter events, 9.3 us)
Async XLA Ops:
  7.2 2.0 copy-start
  7.2 132.4 %all-reduce.12.cloned.1.call-start = ((), (), s32[]{:S(2)}) async-start(), calls=%async_computation.1 | async-start | bytes 8388608 | tf_op jit(solution)/shard_map/psum | solution.py:22
  9.1 8.6 %copy-start.2 = (f32[1024,256]{1,0:T(8,128)S(1)}, f32[1024,256]{1,0:T(8,128)}, u32[]{:S(2)}) copy-start(f32[1024,256]{1,0:T(8,128)} %param.15) | copy-start | bytes 3145732
  26.3 4.5 copy-start.3
  33.5 194.5 %all-reduce.16.cloned.1.call-start = ((), (), s32[]{:S(2)}) async-start(), calls=%async_computation.3 | async-start | bytes 2621440 | tf_op jit(solution)/shard_map/psum | solution.py:28
  139.6 7.8 %copy-start.4 = (f32[2048,256]{1,0:T(8,128)S(1)}, f32[2048,256]{1,0:T(8,128)}, u32[]{:S(2)}) copy-start(f32[2048,256]{1,0:T(8,128)} %get-tuple-element.47) | copy-start | bytes 6291460
  139.6 7.8 %copy-start.5 = (f32[2048,256]{1,0:T(8,128)S(1)}, f32[2048,256]{1,0:T(8,128)}, u32[]{:S(2)}) copy-start(f32[2048,256]{1,0:T(8,128)} %get-tuple-element.48) | copy-start | bytes 6291460
  164.3 281.3 %all-reduce.10.cloned.1.call-start = ((), (), s32[]{:S(2)}) async-start(), calls=%async_computation | async-start | bytes 8388608 | tf_op jit(solution)/shard_map/psum | solution.py:22
  228.0 62.8 %copy-start.8 = (f32[256,1024]{1,0:T(8,128)S(1)}, f32[256,1024]{1,0:T(8,128)}, u32[]{:S(2)}) copy-start(f32[256,1024]{1,0:T(8,128)} %get-tuple-element.51) | copy-start | bytes 3145732
  335.4 8.6 %copy-start.1 = (f32[1024,256]{1,0:T(8,128)}, f32[1024,256]{1,0:T(8,128)S(1)}, u32[]{:S(2)}) copy-start(f32[1024,256]{1,0:T(8,128)S(1)} %copy.14) | copy-start | bytes 3145732
  348.3 186.0 %all-reduce.14.cloned.1.call-start = ((), (), s32[]{:S(2)}) async-start(), calls=%async_computation.2 | async-start | bytes 2621440 | tf_op jit(solution)/shard_map/psum | solution.py:28
  445.6 7.8 %copy-start.6 = (f32[2048,256]{1,0:T(8,128)S(1)}, f32[2048,256]{1,0:T(8,128)}, u32[]{:S(2)}) copy-start(f32[2048,256]{1,0:T(8,128)} %get-tuple-element.45) | copy-start | bytes 6291460
  445.6 7.8 %copy-start.7 = (f32[2048,256]{1,0:T(8,128)S(1)}, f32[2048,256]{1,0:T(8,128)}, u32[]{:S(2)}) copy-start(f32[2048,256]{1,0:T(8,128)} %get-tuple-element.46) | copy-start | bytes 6291460
  534.4 62.8 %copy-start.9 = (f32[256,1024]{1,0:T(8,128)S(1)}, f32[256,1024]{1,0:T(8,128)}, u32[]{:S(2)}) copy-start(f32[256,1024]{1,0:T(8,128)} %get-tuple-element.49) | copy-start | bytes 3145732
  641.3 1.5 copy-start.10
Sparse Core Ops, SparseCore 0:
  33.6 105.9 all-reduce.11
  164.4 63.4 all-reduce.15
  348.4 97.1 all-reduce.9
  470.8 63.4 all-reduce.13
where the time goes:
time: 659 us; the launch traced here: 650 us
  waiting for transfers between devices  321 us (49%)
  other arithmetic  128 us (19%)
  blocking collectives  80.6 us (12%)
  matrix products  58 us (9%)
  local copies, waits for them, and re-layouts  44.5 us (7%)
  between operations  17.3 us (3%)
    psum x2, waiting for transfers between devices, solve_mode(): rows_first, rows_second = lax.psum((picked_first, picked_second), 'row')  197 us
    psum x2, waiting for transfers between devices, solve_mode(): product = lax.psum(partial_product, 'samp')  124 us
    psum x2, blocking collectives, solve_mode(): squares_sum = lax.psum(jnp.sum(solved * solved, axis=0), 'row')  80.6 us
    another operation x14, other arithmetic, solve_mode(): lower_factor = jnp.linalg.cholesky(gram_matrix)  69.2 us
    another operation x5, other arithmetic, solve_mode(): solved = jax.scipy.linalg.cho_solve((lower_factor, True), product.T).T  40.1 us
    dot_general x2, matrix products, solve_mode(): partial_product = jnp.dot(fibres, khatri, precision=lax.Precision.HIGHEST)  34.2 us
    gather x4, local copies, waits for them, and re-layouts, select_rows(): picked = jnp.take(owned, jnp.clip(local_idx, 0, height - 1), axis=0)  32.3 us
    dot_general x2, matrix products, gram_of(): return jnp.dot(khatri.T, khatri, precision=lax.Precision.HIGHEST)  15.6 us
  transfers between devices with their start and end apart: 4, of which 4 were waited for; matrix products, arithmetic and copies ran while one was open for 1% of the time, Pallas kernels for 0%

commit v1 on v0

v1 whole, which is shorter than its diff:
```python
import jax
import jax.numpy as jnp
from jax import lax
from jax.experimental import pallas as pl
from jax.experimental.pallas import tpu as pltpu
from jax.sharding import PartitionSpec as P

F32, BF16 = jnp.float32, jnp.bfloat16
CAP = 16
BLOCK = 128
HIGHEST = lax.Precision.HIGHEST
VMEM = pl.BlockSpec(memory_space=pltpu.VMEM)
CORE = [(i, i ^ 1) for i in range(8)]
ALONG_Z = [[c + 2 * z for z in range(4)] for c in range(2)]


def call(kernel, out, *args, flops=0, size=0, **kwargs):
    return pl.pallas_call(
        kernel,
        out_shape=out,
        in_specs=[VMEM] * len(args),
        out_specs=jax.tree.map(lambda _: VMEM, out),
        cost_estimate=pl.CostEstimate(flops=flops, bytes_accessed=size, transcendentals=0),
        compiler_params=pltpu.CompilerParams(vmem_limit_bytes=40 * 2**20),
        **kwargs,
    )(*args)


def shape(*dims, dtype=F32):
    return jax.ShapeDtypeStruct(dims, dtype)


def dot(a, b, dims=(1, 0)):
    return lax.dot_general(a, b, (((dims[0],), (dims[1],)), ((), ())), precision=HIGHEST, preferred_element_type=F32)


def bf16_dot(a, b):
    return jnp.dot(a, b, preferred_element_type=F32)


def halves(x):
    high = x.astype(BF16)
    return high, (x - high.astype(F32)).astype(BF16)


def pick(onehot, x):
    high, rest = x.astype(BF16), x
    total = bf16_dot(onehot, high)
    for _ in range(2):
        rest = rest - high.astype(F32)
        high = rest.astype(BF16)
        total = total + bf16_dot(onehot, high)
    return total


def slots_of(local, height):
    inside = (local >= 0) & (local < height)
    blocks = local.shape[0]
    before = lax.broadcasted_iota(jnp.int32, (BLOCK, BLOCK), 0) < lax.broadcasted_iota(jnp.int32, (BLOCK, BLOCK), 1)
    slot = bf16_dot(jnp.where(inside, 1.0, 0.0).astype(BF16), jnp.where(before, 1.0, 0.0).astype(BF16))
    slot = jnp.where(inside, slot.astype(jnp.int32), -1)
    which = lax.broadcasted_iota(jnp.int32, (blocks, CAP, BLOCK), 1)
    wanted = jnp.where(slot[:, None, :] == which, local[:, None, :] + 1, 0)
    row = jnp.sum(wanted.astype(F32), axis=2, keepdims=True).astype(jnp.int32).reshape(blocks * CAP, 1) - 1
    return jnp.where(row == lax.broadcasted_iota(jnp.int32, (blocks * CAP, height), 1), 1.0, 0.0).astype(BF16)


def select_kernel(columns, index_ref, *refs):
    owned, out_ref = refs[:-1], refs[-1]
    for n, (column, rows) in enumerate(zip(columns, owned)):
        height = rows.shape[0]
        onehot = slots_of(index_ref[column] - lax.axis_index("row") * height, height)
        picked = pick(onehot, rows[...])
        out_ref[:, n * CAP : (n + 1) * CAP, :] = picked.reshape(-1, CAP, picked.shape[-1])


def select(index, columns, *owned):
    blocks, rank = index.shape[1], owned[0].shape[1]
    n = len(columns)
    return call(
        lambda *refs: select_kernel(columns, *refs),
        shape(blocks, n * CAP, rank),
        index,
        *owned,
        flops=n * 6 * blocks * CAP * owned[0].shape[0] * rank,
        size=n * 2**21,
    )


def place_of(index, height):
    eye = lax.broadcasted_iota(jnp.int32, (BLOCK, BLOCK), 0) == lax.broadcasted_iota(jnp.int32, (BLOCK, BLOCK), 1)
    before = lax.broadcasted_iota(jnp.int32, (BLOCK, BLOCK), 1) < lax.broadcasted_iota(jnp.int32, (BLOCK, BLOCK), 0)
    owner = lax.shift_right_logical(index, height.bit_length() - 1)
    owner = jnp.broadcast_to(owner.astype(F32), (BLOCK, BLOCK))
    column = jnp.sum(jnp.where(eye, owner, 0.0), axis=1, keepdims=True)
    slot = jnp.sum(jnp.where((owner == column) & before, 1.0, 0.0), axis=1, keepdims=True)
    return column.astype(jnp.int32), slot.astype(jnp.int32)


def placed_rows(index, got, which, height):
    owners, slots, rank = got.shape
    owner, slot = place_of(index, height)
    target = owner * slots + which * CAP + slot
    onehot = target == lax.broadcasted_iota(jnp.int32, (BLOCK, owners * slots), 1)
    return pick(jnp.where(onehot, 1.0, 0.0).astype(BF16), got.reshape(owners * slots, rank))


def spread(out_ref, block):
    for peer in range(out_ref.shape[0]):
        out_ref[peer] = block


def first_khatri_kernel(height, index_ref, got_ref, out_ref):
    me = pl.ds(lax.axis_index("row"), 1)
    got = got_ref[...]
    rows = [placed_rows(index_ref[c, me, :], got, c, height) for c in range(2)]
    spread(out_ref, rows[0] * rows[1])


def second_khatri_kernel(height, index_ref, got_ref, other_ref, inverse_ref, scale_ref, out_ref):
    me = pl.ds(lax.axis_index("row"), 1)
    rows = placed_rows(index_ref[0, me, :], got_ref[...], 0, height)
    other = placed_rows(index_ref[1, me, :], other_ref[...], 0, height)
    rows = dot(rows, inverse_ref[...]) / scale_ref[...]
    spread(out_ref, rows * other)


def gram_kernel(khatri_ref, out_ref, gram):
    high, low = halves(khatri_ref[...])
    t = lambda a, b: lax.dot_general(a, b, (((0,), (0,)), ((), ())), preferred_element_type=F32)
    cross = t(high, low)
    gram[...] = t(high, high) + (cross + cross.T)
    mine = out_ref.shape[1]
    block = gram[pl.ds(pl.multiple_of(lax.axis_index("row") * mine, mine), mine), :]
    spread(out_ref, block)


def invert_block(tiles):
    n = len(tiles)
    sub = lax.broadcasted_iota(jnp.int32, (8, 128), 0)
    lane = lax.broadcasted_iota(jnp.int32, (8, 128), 1)
    wide = lambda part: jnp.broadcast_to(part, (8, 128))
    for j in range(n):
        t = tiles[j]
        cols = [wide(t[:, 8 * j + k : 8 * j + k + 1]) for k in range(8)]
        in_panel = (lane >= 8 * j) & (lane < 8 * j + 8)
        rows = jnp.where(in_panel, jnp.where(lane == sub + 8 * j, 1.0, 0.0), t)
        for k in range(8):
            inverse = 1.0 / wide(cols[k][k : k + 1, :])
            here = sub == k
            factor = jnp.where(here, 0.0, cols[k])
            row = wide(rows[k : k + 1, :]) * inverse
            rows = jnp.where(here, row, rows - factor * row)
            for m in range(k + 1, 8):
                entry = wide(cols[m][k : k + 1, :]) * inverse
                cols[m] = jnp.where(here, entry, cols[m] - factor * entry)
        spread_rows = [wide(rows[k : k + 1, :]) for k in range(8)]
        for i in range(n):
            if i != j:
                t = tiles[i]
                kept = jnp.where(in_panel, 0.0, t)
                for k in range(8):
                    kept = kept - wide(t[:, 8 * j + k : 8 * j + k + 1]) * spread_rows[k]
                tiles[i] = kept
        tiles[j] = rows
    return jnp.concatenate(tiles, axis=0)


def inverse_kernel(gram_ref, out_ref):
    h = gram_ref.shape[0] // 2
    a = invert_block([gram_ref[8 * i : 8 * i + 8, :h] for i in range(h // 8)])
    w = dot(a, gram_ref[:h, h:])
    out_ref[h:, h:] = gram_ref[h:, h:] - dot(gram_ref[h:, :h], w)
    s = invert_block([out_ref[h + 8 * i : h + 8 * i + 8, h:] for i in range(h // 8)])
    ws = dot(w, s)
    out_ref[h:, h:] = s
    out_ref[:h, h:] = -ws
    out_ref[h:, :h] = -ws.T
    out_ref[:h, :h] = a + dot(ws, w, (1, 1))


def gram_inverse(khatri):
    rank = khatri.shape[1]
    mine = rank // 16
    slices = call(
        gram_kernel,
        shape(8, mine, rank),
        khatri,
        scratch_shapes=[pltpu.VMEM((rank, rank), F32)],
        flops=6 * khatri.size * rank,
        size=4 * khatri.size,
    )
    parts = lax.all_to_all(slices, "samp", 0, 0, tiled=True)
    summed = jnp.broadcast_to(jnp.sum(parts, axis=0)[None], (16, mine, rank))
    gram = lax.all_to_all(summed, "row", 0, 0, tiled=True).reshape(rank, rank)
    return call(inverse_kernel, shape(rank, rank), gram, flops=2 * 10**10, size=2**19)


def product_kernel(fibres_ref, khatri_ref, out_ref, high_ref, low_ref):
    @pl.when(pl.program_id(0) == 0)
    def _():
        high_ref[...], low_ref[...] = halves(khatri_ref[...])

    high, low = halves(fibres_ref[...])
    out_ref[...] = bf16_dot(high, high_ref[...]) + (bf16_dot(high, low_ref[...]) + bf16_dot(low, high_ref[...]))


def product(fibres, khatri, half):
    rows, depth = fibres.shape
    rank = khatri.shape[1]
    steps = rows // 2 // BLOCK
    grid = pltpu.PrefetchScalarGridSpec(
        num_scalar_prefetch=1,
        grid=(steps,),
        in_specs=[
            pl.BlockSpec((BLOCK, depth), lambda i, h: (h[0] * steps + i, 0)),
            pl.BlockSpec((depth, rank), lambda i, h: (0, 0)),
        ],
        out_specs=pl.BlockSpec((BLOCK, rank), lambda i, h: (i, 0)),
        scratch_shapes=[pltpu.VMEM((depth, rank), BF16)] * 2,
    )
    return pl.pallas_call(
        lambda half_ref, *refs: product_kernel(*refs),
        grid_spec=grid,
        out_shape=shape(rows // 2, rank),
        cost_estimate=pl.CostEstimate(flops=6 * rows // 2 * depth * rank, bytes_accessed=2 * rows * depth, transcendentals=0),
        compiler_params=pltpu.CompilerParams(vmem_limit_bytes=40 * 2**20),
    )(half.reshape(1), fibres, khatri)


def summed_product(fibres, khatri):
    core = lax.axis_index("samp") % 2
    given = lax.ppermute(product(fibres, khatri, 1 - core), "samp", CORE)
    kept = product(fibres, khatri, core) + given
    quarters = lax.all_to_all(kept.reshape(4, -1, kept.shape[1]), "samp", 0, 0, axis_index_groups=ALONG_Z, tiled=True)
    mine = jnp.sum(quarters, axis=0)
    own = lax.all_to_all(
        jnp.broadcast_to(mine[None], quarters.shape), "samp", 0, 0, axis_index_groups=ALONG_Z, tiled=True
    ).reshape(kept.shape)
    other = lax.ppermute(own, "samp", CORE)
    return jnp.concatenate([jnp.where(core == 0, own, other), jnp.where(core == 0, other, own)])


def solve_kernel(product_ref, inverse_ref, solved_ref, squares_ref):
    solved = dot(product_ref[...], inverse_ref[...])
    solved_ref[...] = solved
    squares_ref[...] = jnp.broadcast_to(jnp.sum(solved * solved, axis=0, keepdims=True), squares_ref.shape)


def solve(total, inverse):
    rows, rank = total.shape
    solved, squares = call(
        solve_kernel,
        (shape(rows, rank), shape(16, rank)),
        total,
        inverse,
        flops=12 * rows * rank * rank,
        size=8 * rows * rank,
    )
    squares = lax.all_to_all(squares, "row", 0, 0, tiled=True)
    return solved, jnp.sqrt(jnp.sum(squares, axis=0, keepdims=True) / (16 * rows) + 1e-6)


def exchange(rows):
    return lax.all_to_all(rows, "row", 0, 0, tiled=True)


def shards(fibres_first, fibres_second, index_first, index_second, factor_b, factor_c):
    height, rank = factor_b.shape
    by_block = lambda index: index.T.reshape(2, 16, BLOCK)
    first, second = by_block(index_first), by_block(index_second)

    got = exchange(select(first, (0, 1), factor_b, factor_c))
    blocks = call(lambda *refs: first_khatri_kernel(height, *refs), shape(16, BLOCK, rank), first, got, flops=10**8, size=2**22)
    khatri = exchange(blocks).reshape(-1, rank)
    inverse = gram_inverse(khatri)
    total = summed_product(fibres_first, khatri)
    solved, scale = solve(total, inverse)
    factor_a = solved / scale

    other = exchange(select(second, (1,), factor_c))
    got = exchange(select(second, (0,), total))
    blocks = call(
        lambda *refs: second_khatri_kernel(height, *refs),
        shape(16, BLOCK, rank),
        second,
        got,
        other,
        inverse,
        scale,
        flops=10**8,
        size=2**22,
    )
    khatri = exchange(blocks).reshape(-1, rank)
    inverse = gram_inverse(khatri)
    total = summed_product(fibres_second, khatri)
    solved, weights = solve(total, inverse)
    return (factor_a, solved / weights, weights.reshape(rank))


def solution(mesh):
    placed = (P("row", "samp"), P("row", "samp"), P("samp", None), P("samp", None), P("row", None), P("row", None))
    return jax.shard_map(
        shards,
        mesh=mesh,
        in_specs=placed,
        out_specs=(P("row", None), P("row", None), P()),
        check_vma=False,
    )
```

time: 659 us -> 277 us (0.42); the launches traced: 650 us -> 276 us
  waiting for transfers between devices: 321 us -> 114 us
  other arithmetic: 128 us -> 5.36 us
  matrix products: 58 us -> 0 us
  starting transfers between devices: 0.38 us -> 52.1 us
  Pallas kernels: 0 us -> 39.6 us
  blocking collectives: 80.6 us -> 45 us
  local copies, waits for them, and re-layouts: 44.5 us -> 19 us
  between operations: 17.3 us -> 1 us
    psum x4 -> x0, waiting for transfers between devices: 321 us -> none  [the longest x2 197 us: solve_mode(): rows_first, rows_second = lax.psum((picked_first, picked_second), 'row')]
    all_to_all x0 -> x13, waiting for transfers between devices: none -> 114 us  [the longest x3 38.1 us: exchange(): return lax.all_to_all(rows, 'row', 0, 0, tiled=True)]
    another operation x19 -> x0, other arithmetic: 109 us -> none  [the longest x14 69.2 us: solve_mode(): lower_factor = jnp.linalg.cholesky(gram_matrix)]
    psum x2 -> x0, blocking collectives: 80.6 us -> none  [solve_mode(): squares_sum = lax.psum(jnp.sum(solved * solved, axis=0), 'row')]
    all_to_all x0 -> x13, starting transfers between devices: none -> 51.6 us  [the longest x3 11 us: exchange(): return lax.all_to_all(rows, 'row', 0, 0, tiled=True)]
    dot_general x4 -> x0, matrix products: 49.8 us -> none  [the longest x2 34.2 us: solve_mode(): partial_product = jnp.dot(fibres, khatri, precision=lax.Precision.HIGHEST)]
    all_to_all x0 -> x2, blocking collectives: none -> 45 us  [exchange(): return lax.all_to_all(rows, 'row', 0, 0, tiled=True)]
    pallas_call x0 -> x15, Pallas kernels: none -> 39.6 us  [the longest x11 28.8 us: call(): pl.pallas_call(kernel, out_shape=out, in_specs=[VMEM] * len(args), out_sp...]
  transfers between devices with their start and end apart: 4 -> 17, of which waited for: 4 -> 12; matrix products, arithmetic and copies ran while one was open for 1% -> 1% of each run, Pallas kernels for 0% -> 11%
where the time goes in v1:
time: 277 us; the launch traced here: 276 us
  waiting for transfers between devices  114 us (41%)
  starting transfers between devices  52.1 us (19%)
  blocking collectives  45 us (16%)
  Pallas kernels  39.6 us (14%)
  local copies, waits for them, and re-layouts  19 us (7%)
  other arithmetic  5.36 us (2%)
    all_to_all x2, blocking collectives, exchange(): return lax.all_to_all(rows, 'row', 0, 0, tiled=True)  45 us
    all_to_all x3, waiting for transfers between devices, exchange(): return lax.all_to_all(rows, 'row', 0, 0, tiled=True)  38.1 us
    pallas_call x11, Pallas kernels, call(): pl.pallas_call(kernel, out_shape=out, in_specs=[VMEM] * len(args), out_sp...  28.8 us
    all_to_all x2, waiting for transfers between devices, summed_product(): lax.all_to_all(jnp.broadcast_to(mine[None], quarters.shape), 'samp', 0, 0...  19 us
    all_to_all x2, waiting for transfers between devices, summed_product(): lax.all_to_all(kept.reshape(4, -1, kept.shape[1]), 'samp', 0, 0, axis_ind...  17.6 us
    all_to_all x2, waiting for transfers between devices, gram_inverse(): gram = lax.all_to_all(summed, 'row', 0, 0, tiled=True).reshape(rank, rank)  15.7 us
    unnamed x20, local copies, waits for them, and re-layouts  14.6 us
    all_to_all x2, waiting for transfers between devices, solve(): squares = lax.all_to_all(squares, 'row', 0, 0, tiled=True)  12.5 us
  transfers between devices with their start and end apart: 17, of which 12 were waited for; matrix products, arithmetic and copies ran while one was open for 1% of the time, Pallas kernels for 11%

profile of v1, /device:TPU:0, one launch (start us, length us, event | category | flops | bytes accessed | tf_op | source)
XLA Modules:
  0.0 276.0 jit_solution(11476993859993257072)
XLA Ops:
  1.4 1.2 copy-done.4
  2.6 1.2 copy-done.5
  3.8 1.3 shard_map.85
  5.1 18.5 %all_to_all.83.refs_1_ = f32[16,32,256]{2,1,0:T(8,128)S(1)} all-to-all(f32[16,32,256]{2,1,0:T(8,128)S(1)} %shard_map.85), channel_id=1, replica_groups=mesh['row'=16,'samp'=8] {'row'}, dimensions={0} | all-to-all | bytes 1048576 | tf_op jit(solution)/shard_map/all_to_all | solution.py:265
  24.3 1.3 copy-done.3
  25.6 3.7 %all-to-all-start.1 = ((f32[16,128,256]{2,1,0:T(8,128)}), f32[16,128,256]{2,1,0:T(8,128)S(1)}, u32[]{:S(2)}, u32[]{:S(2)}) async-start(f32[16,128,256]{2,1,0:T(8,128)} %copy-done.3), calls=%async_computation.1 | async-start | bytes 4194304 | tf_op jit(solution)/shard_map/all_to_all | solution.py:265
  29.4 29.5 %all-to-all-done.1 = f32[16,128,256]{2,1,0:T(8,128)S(1)} async-done(((f32[16,128,256]{2,1,0:T(8,128)}), f32[16,128,256]{2,1,0:T(8,128)S(1)}, u32[]{:S(2)}, u32[]{:S(2)}) %all-to-all-start.1) | async-done | bytes 2097184 | tf_op jit(solution)/shard_map/all_to_all | solution.py:265
  58.9 3.4 %copy-done = f32[1024,2048]{1,0:T(8,128)S(1)} copy-done((f32[1024,2048]{1,0:T(8,128)S(1)}, f32[1024,2048]{1,0:T(8,128)}, u32[]{:S(2)}) %copy-start) | copy-done | bytes 8388632
  62.3 2.7 shard_map.88
  65.0 3.4 %copy-done.1 = f32[1024,2048]{1,0:T(8,128)S(1)} copy-done((f32[1024,2048]{1,0:T(8,128)S(1)}, f32[1024,2048]{1,0:T(8,128)}, u32[]{:S(2)}) %copy-start.1) | copy-done | bytes 8388632
  68.4 2.7 shard_map.87
  72.0 5.3 %all-to-all-start.2 = ((f32[4,128,256]{2,1,0:T(8,128)}), f32[4,128,256]{2,1,0:T(8,128)S(1)}, u32[]{:S(2)}, u32[]{:S(2)}) async-start(f32[4,128,256]{2,1,0:T(8,128)} %bitcast.4), calls=%async_computation.2 | async-start | bytes 1048576 | tf_op jit(solution)/shard_map/all_to_all | solution.py:235
  77.3 1.5 shard_map.89
  78.7 8.7 %all-to-all-done.2 = f32[4,128,256]{2,1,0:T(8,128)S(1)} async-done(((f32[4,128,256]{2,1,0:T(8,128)}), f32[4,128,256]{2,1,0:T(8,128)S(1)}, u32[]{:S(2)}, u32[]{:S(2)}) %all-to-all-start.2) | async-done | bytes 524320 | tf_op jit(solution)/shard_map/all_to_all | solution.py:235
  87.4 3.4 %all-to-all-start.4 = ((f32[8,16,256]{2,1,0:T(8,128)}), f32[8,16,256]{2,1,0:T(8,128)S(1)}, u32[]{:S(2)}, u32[]{:S(2)}) async-start(f32[8,16,256]{2,1,0:T(8,128)} %shard_map.89), calls=%async_computation.4 | async-start | bytes 262144 | tf_op jit(solution)/shard_map/all_to_all | solution.py:193
  90.8 6.0 %all-to-all-done.4 = f32[8,16,256]{2,1,0:T(8,128)S(1)} async-done(((f32[8,16,256]{2,1,0:T(8,128)}), f32[8,16,256]{2,1,0:T(8,128)S(1)}, u32[]{:S(2)}, u32[]{:S(2)}) %all-to-all-start.4) | async-done | bytes 131104 | tf_op jit(solution)/shard_map/all_to_all | solution.py:193
  97.7 3.5 %all-to-all-start.3 = ((f32[4,128,256]{2,1,0:T(8,128)}), f32[4,128,256]{2,1,0:T(8,128)S(1)}, u32[]{:S(2)}, u32[]{:S(2)}) async-start(f32[4,128,256]{2,1,0:T(8,128)} %broadcast_in_dim.8), calls=%async_computation.3 | async-start | bytes 1048576 | tf_op jit(solution)/shard_map/all_to_all | solution.py:237
  101.2 9.5 %all-to-all-done.3 = f32[4,128,256]{2,1,0:T(8,128)S(1)} async-done(((f32[4,128,256]{2,1,0:T(8,128)}), f32[4,128,256]{2,1,0:T(8,128)S(1)}, u32[]{:S(2)}, u32[]{:S(2)}) %all-to-all-start.3) | async-done | bytes 524320 | tf_op jit(solution)/shard_map/all_to_all | solution.py:237
  111.4 3.5 %all-to-all-start.5 = ((f32[16,16,256]{2,1,0:T(8,128)}), f32[16,16,256]{2,1,0:T(8,128)S(1)}, u32[]{:S(2)}, u32[]{:S(2)}) async-start(f32[16,16,256]{2,1,0:T(8,128)} %broadcast_in_dim.9), calls=%async_computation.5 | async-start | bytes 524288 | tf_op jit(solution)/shard_map/all_to_all | solution.py:195
  115.0 1.5 shard_map.93
  116.5 7.1 %all-to-all-done.5 = f32[16,16,256]{2,1,0:T(8,128)S(1)} async-done(((f32[16,16,256]{2,1,0:T(8,128)}), f32[16,16,256]{2,1,0:T(8,128)S(1)}, u32[]{:S(2)}, u32[]{:S(2)}) %all-to-all-start.5) | async-done | bytes 262176 | tf_op jit(solution)/shard_map/all_to_all | solution.py:195
  123.6 3.7 %all-to-all-start.8 = ((f32[16,16,256]{2,1,0:T(8,128)}), f32[16,16,256]{2,1,0:T(8,128)S(1)}, u32[]{:S(2)}, u32[]{:S(2)}) async-start(f32[16,16,256]{2,1,0:T(8,128)} %shard_map.93), calls=%async_computation.8 | async-start | bytes 524288 | tf_op jit(solution)/shard_map/all_to_all | solution.py:265
  127.3 9.0 %shard_map.90.inverse_ref.refs_3_ = f32[256,256]{1,0:T(8,128)S(1)} custom-call(f32[256,256]{1,0:T(8,128)S(1)} %bitcast.33), custom_call_target="tpu_custom_call" | custom-call | flops 20000000000 | bytes 524288 | tf_op jit(solution)/shard_map/pallas_call | solution.py:18
  136.5 1.0 shard_map.91
  138.1 7.0 %all-to-all-start.6 = ((f32[16,1,256]{2,1,0:T(1,128)}), f32[16,1,256]{2,1,0:T(1,128)S(1)}, u32[]{:S(2)}, u32[]{:S(2)}) async-start(f32[16,1,256]{2,1,0:T(1,128)} %copy.9), calls=%async_computation.6 | async-start | bytes 32768 | tf_op jit(solution)/shard_map/all_to_all | solution.py:260
  145.1 1.5 shard_map.92
  146.6 6.1 %all-to-all-done.6 = f32[16,1,256]{2,1,0:T(1,128)S(1)} async-done(((f32[16,1,256]{2,1,0:T(1,128)}), f32[16,1,256]{2,1,0:T(1,128)S(1)}, u32[]{:S(2)}, u32[]{:S(2)}) %all-to-all-start.6) | async-done | bytes 16416 | tf_op jit(solution)/shard_map/all_to_all | solution.py:260
  152.7 3.5 %all-to-all-start.7 = ((f32[16,16,256]{2,1,0:T(8,128)}), f32[16,16,256]{2,1,0:T(8,128)S(1)}, u32[]{:S(2)}, u32[]{:S(2)}) async-start(f32[16,16,256]{2,1,0:T(8,128)} %shard_map.92), calls=%async_computation.7 | async-start | bytes 524288 | tf_op jit(solution)/shard_map/all_to_all | solution.py:265
  156.3 8.6 %all-to-all-done.7.refs_1_ = f32[16,16,256]{2,1,0:T(8,128)S(1)} async-done(((f32[16,16,256]{2,1,0:T(8,128)}), f32[16,16,256]{2,1,0:T(8,128)S(1)}, u32[]{:S(2)}, u32[]{:S(2)}) %all-to-all-start.7) | async-done | bytes 262176 | tf_op jit(solution)/shard_map/all_to_all | solution.py:265
  165.7 26.6 %all_to_all.84 = f32[16,128,256]{2,1,0:T(8,128)S(1)} all-to-all(f32[16,128,256]{2,1,0:T(8,128)S(1)} %shard_map.94), channel_id=1, replica_groups=mesh['row'=16,'samp'=8] {'row'}, dimensions={0} | all-to-all | bytes 4194304 | tf_op jit(solution)/shard_map/all_to_all | solution.py:265
  192.3 3.4 %copy-done.2 = f32[1024,2048]{1,0:T(8,128)S(1)} copy-done((f32[1024,2048]{1,0:T(8,128)S(1)}, f32[1024,2048]{1,0:T(8,128)}, u32[]{:S(2)}) %copy-start.2) | copy-done | bytes 8388632
  195.7 2.7 shard_map.96
  198.7 2.7 shard_map.95
  202.3 4.1 %all-to-all-start.10 = ((f32[4,128,256]{2,1,0:T(8,128)}), f32[4,128,256]{2,1,0:T(8,128)}, u32[]{:S(2)}, u32[]{:S(2)}) async-start(f32[4,128,256]{2,1,0:T(8,128)} %bitcast.45), calls=%async_computation.10 | async-start | bytes 1048576 | tf_op jit(solution)/shard_map/all_to_all | solution.py:235
  206.5 1.5 shard_map.97
  207.9 9.0 %all-to-all-done.10 = f32[4,128,256]{2,1,0:T(8,128)} async-done(((f32[4,128,256]{2,1,0:T(8,128)}), f32[4,128,256]{2,1,0:T(8,128)}, u32[]{:S(2)}, u32[]{:S(2)}) %all-to-all-start.10) | async-done | bytes 524320 | tf_op jit(solution)/shard_map/all_to_all | solution.py:235
  216.9 3.4 %all-to-all-start.12 = ((f32[8,16,256]{2,1,0:T(8,128)}), f32[8,16,256]{2,1,0:T(8,128)S(1)}, u32[]{:S(2)}, u32[]{:S(2)}) async-start(f32[8,16,256]{2,1,0:T(8,128)} %shard_map.97), calls=%async_computation.12 | async-start | bytes 262144 | tf_op jit(solution)/shard_map/all_to_all | solution.py:193
  220.3 1.1 reduce_sum.57
  221.4 5.0 %all-to-all-done.12 = f32[8,16,256]{2,1,0:T(8,128)S(1)} async-done(((f32[8,16,256]{2,1,0:T(8,128)}), f32[8,16,256]{2,1,0:T(8,128)S(1)}, u32[]{:S(2)}, u32[]{:S(2)}) %all-to-all-start.12) | async-done | bytes 131104 | tf_op jit(solution)/shard_map/all_to_all | solution.py:193
  227.2 3.5 %all-to-all-start.11 = ((f32[4,128,256]{2,1,0:T(8,128)}), f32[4,128,256]{2,1,0:T(8,128)S(1)}, u32[]{:S(2)}, u32[]{:S(2)}) async-start(f32[4,128,256]{2,1,0:T(8,128)} %broadcast_in_dim.10), calls=%async_computation.11 | async-start | bytes 1048576 | tf_op jit(solution)/shard_map/all_to_all | solution.py:237
  230.7 9.5 %all-to-all-done.11 = f32[4,128,256]{2,1,0:T(8,128)S(1)} async-done(((f32[4,128,256]{2,1,0:T(8,128)}), f32[4,128,256]{2,1,0:T(8,128)S(1)}, u32[]{:S(2)}, u32[]{:S(2)}) %all-to-all-start.11) | async-done | bytes 524320 | tf_op jit(solution)/shard_map/all_to_all | solution.py:237
  240.9 3.5 %all-to-all-start.13 = ((f32[16,16,256]{2,1,0:T(8,128)}), f32[16,16,256]{2,1,0:T(8,128)S(1)}, u32[]{:S(2)}, u32[]{:S(2)}) async-start(f32[16,16,256]{2,1,0:T(8,128)} %broadcast_in_dim.11), calls=%async_computation.13 | async-start | bytes 524288 | tf_op jit(solution)/shard_map/all_to_all | solution.py:195
  244.5 8.6 %all-to-all-done.13 = f32[16,16,256]{2,1,0:T(8,128)S(1)} async-done(((f32[16,16,256]{2,1,0:T(8,128)}), f32[16,16,256]{2,1,0:T(8,128)S(1)}, u32[]{:S(2)}, u32[]{:S(2)}) %all-to-all-start.13) | async-done | bytes 262176 | tf_op jit(solution)/shard_map/all_to_all | solution.py:195
  253.1 9.0 %shard_map.98.inverse_ref = f32[256,256]{1,0:T(8,128)S(1)} custom-call(f32[256,256]{1,0:T(8,128)S(1)} %bitcast.34), custom_call_target="tpu_custom_call" | custom-call | flops 20000000000 | bytes 524288 | tf_op jit(solution)/shard_map/pallas_call | solution.py:18
  263.9 3.5 %all-to-all-start.14 = ((f32[16,1,256]{2,1,0:T(1,128)}), f32[16,1,256]{2,1,0:T(1,128)S(1)}, u32[]{:S(2)}, u32[]{:S(2)}) async-start(f32[16,1,256]{2,1,0:T(1,128)} %copy.10), calls=%async_computation.14 | async-start | bytes 32768 | tf_op jit(solution)/shard_map/all_to_all | solution.py:260
  267.4 1.0 broadcast_divide_fusion.1
  268.4 6.5 %all-to-all-done.14 = f32[16,1,256]{2,1,0:T(1,128)S(1)} async-done(((f32[16,1,256]{2,1,0:T(1,128)}), f32[16,1,256]{2,1,0:T(1,128)S(1)}, u32[]{:S(2)}, u32[]{:S(2)}) %all-to-all-start.14) | async-done | bytes 16416 | tf_op jit(solution)/shard_map/all_to_all | solution.py:260
  275.0 1.0 broadcast_divide_fusion
  (45 shorter events, 10.3 us)
Async XLA Ops:
  1.4 1.2 copy-start.4
  2.6 1.2 copy-start.5
  24.3 1.3 copy-start.3
  25.6 33.3 %all-to-all-start.1 = ((f32[16,128,256]{2,1,0:T(8,128)}), f32[16,128,256]{2,1,0:T(8,128)S(1)}, u32[]{:S(2)}, u32[]{:S(2)}) async-start(f32[16,128,256]{2,1,0:T(8,128)} %copy-done.3), calls=%async_computation.1 | async-start | bytes 4194304 | tf_op jit(solution)/shard_map/all_to_all | solution.py:265
  58.9 3.4 %copy-start = (f32[1024,2048]{1,0:T(8,128)S(1)}, f32[1024,2048]{1,0:T(8,128)}, u32[]{:S(2)}) copy-start(f32[1024,2048]{1,0:T(8,128)} %refs_0_.5) | copy-start | bytes 25165828
  64.9 6.1 %collective-permute-start = (f32[512,256]{1,0:T(8,128)S(1)}, f32[512,256]{1,0:T(8,128)S(1)}, u32[]{:S(2)}, u32[]{:S(2)}) collective-permute-start(f32[512,256]{1,0:T(8,128)S(1)} %shard_map.88), channel_id=1, source_target_pairs={{0,1},{1,0},{2,3},{3,2},{4,5},{5,4},{6,7},{7,6},{8,9},{9,8},{10,11... | collective-permute-start | bytes 1572872 | tf_op jit(solution)/shard_map/ppermute | solution.py:233
  65.0 3.4 %copy-start.1 = (f32[1024,2048]{1,0:T(8,128)S(1)}, f32[1024,2048]{1,0:T(8,128)}, u32[]{:S(2)}) copy-start(f32[1024,2048]{1,0:T(8,128)} %refs_0_.5) | copy-start | bytes 25165828
  72.0 15.4 %all-to-all-start.2 = ((f32[4,128,256]{2,1,0:T(8,128)}), f32[4,128,256]{2,1,0:T(8,128)S(1)}, u32[]{:S(2)}, u32[]{:S(2)}) async-start(f32[4,128,256]{2,1,0:T(8,128)} %bitcast.4), calls=%async_computation.2 | async-start | bytes 1048576 | tf_op jit(solution)/shard_map/all_to_all | solution.py:235
  78.7 36.2 %copy-start.7 = (s32[2048,2]{0,1:T(2,128)S(1)}, s32[2048,2]{0,1:T(2,128)}, u32[]{:S(2)}) copy-start(s32[2048,2]{0,1:T(2,128)} %param.9) | copy-start | bytes 49156
  78.7 36.2 %copy-start.6 = (f32[1024,256]{1,0:T(8,128)S(1)}, f32[1024,256]{1,0:T(8,128)}, u32[]{:S(2)}) copy-start(f32[1024,256]{1,0:T(8,128)} %refs_1_.3) | copy-start | bytes 3145732
  87.4 9.4 %all-to-all-start.4 = ((f32[8,16,256]{2,1,0:T(8,128)}), f32[8,16,256]{2,1,0:T(8,128)S(1)}, u32[]{:S(2)}, u32[]{:S(2)}) async-start(f32[8,16,256]{2,1,0:T(8,128)} %shard_map.89), calls=%async_computation.4 | async-start | bytes 262144 | tf_op jit(solution)/shard_map/all_to_all | solution.py:193
  97.7 13.0 %all-to-all-start.3 = ((f32[4,128,256]{2,1,0:T(8,128)}), f32[4,128,256]{2,1,0:T(8,128)S(1)}, u32[]{:S(2)}, u32[]{:S(2)}) async-start(f32[4,128,256]{2,1,0:T(8,128)} %broadcast_in_dim.8), calls=%async_computation.3 | async-start | bytes 1048576 | tf_op jit(solution)/shard_map/all_to_all | solution.py:237
  111.4 12.2 %all-to-all-start.5 = ((f32[16,16,256]{2,1,0:T(8,128)}), f32[16,16,256]{2,1,0:T(8,128)S(1)}, u32[]{:S(2)}, u32[]{:S(2)}) async-start(f32[16,16,256]{2,1,0:T(8,128)} %broadcast_in_dim.9), calls=%async_computation.5 | async-start | bytes 524288 | tf_op jit(solution)/shard_map/all_to_all | solution.py:195
  116.5 19.8 %collective-permute-start.1 = (f32[512,256]{1,0:T(8,128)S(1)}, f32[512,256]{1,0:T(8,128)S(1)}, u32[]{:S(2)}, u32[]{:S(2)}) collective-permute-start(f32[512,256]{1,0:T(8,128)S(1)} %bitcast.43), channel_id=1, source_target_pairs={{0,1},{1,0},{2,3},{3,2},{4,5},{5,4},{6,7},{7,6},{8,9},{9,8},{10,11... | collective-permute-start | bytes 1572872 | tf_op jit(solution)/shard_map/ppermute | solution.py:240
  123.6 14.5 %all-to-all-start.8 = ((f32[16,16,256]{2,1,0:T(8,128)}), f32[16,16,256]{2,1,0:T(8,128)S(1)}, u32[]{:S(2)}, u32[]{:S(2)}) async-start(f32[16,16,256]{2,1,0:T(8,128)} %shard_map.93), calls=%async_computation.8 | async-start | bytes 524288 | tf_op jit(solution)/shard_map/all_to_all | solution.py:265
  138.1 14.6 %all-to-all-start.6 = ((f32[16,1,256]{2,1,0:T(1,128)}), f32[16,1,256]{2,1,0:T(1,128)S(1)}, u32[]{:S(2)}, u32[]{:S(2)}) async-start(f32[16,1,256]{2,1,0:T(1,128)} %copy.9), calls=%async_computation.6 | async-start | bytes 32768 | tf_op jit(solution)/shard_map/all_to_all | solution.py:260
  152.7 12.2 %all-to-all-start.7 = ((f32[16,16,256]{2,1,0:T(8,128)}), f32[16,16,256]{2,1,0:T(8,128)S(1)}, u32[]{:S(2)}, u32[]{:S(2)}) async-start(f32[16,16,256]{2,1,0:T(8,128)} %shard_map.92), calls=%async_computation.7 | async-start | bytes 524288 | tf_op jit(solution)/shard_map/all_to_all | solution.py:265
  192.3 3.4 %copy-start.2 = (f32[1024,2048]{1,0:T(8,128)S(1)}, f32[1024,2048]{1,0:T(8,128)}, u32[]{:S(2)}) copy-start(f32[1024,2048]{1,0:T(8,128)} %refs_0_.7) | copy-start | bytes 25165828
  198.4 3.0 %collective-permute-start.2 = (f32[512,256]{1,0:T(8,128)S(1)}, f32[512,256]{1,0:T(8,128)S(1)}, u32[]{:S(2)}, u32[]{:S(2)}) collective-permute-start(f32[512,256]{1,0:T(8,128)S(1)} %shard_map.96), channel_id=1, source_target_pairs={{0,1},{1,0},{2,3},{3,2},{4,5},{5,4},{6,7},{7,6},{8,9},{9,8},{10,11... | collective-permute-start | bytes 1572872 | tf_op jit(solution)/shard_map/ppermute | solution.py:233
  202.3 14.6 %all-to-all-start.10 = ((f32[4,128,256]{2,1,0:T(8,128)}), f32[4,128,256]{2,1,0:T(8,128)}, u32[]{:S(2)}, u32[]{:S(2)}) async-start(f32[4,128,256]{2,1,0:T(8,128)} %bitcast.45), calls=%async_computation.10 | async-start | bytes 1048576 | tf_op jit(solution)/shard_map/all_to_all | solution.py:235
  216.9 9.4 %all-to-all-start.12 = ((f32[8,16,256]{2,1,0:T(8,128)}), f32[8,16,256]{2,1,0:T(8,128)S(1)}, u32[]{:S(2)}, u32[]{:S(2)}) async-start(f32[8,16,256]{2,1,0:T(8,128)} %shard_map.97), calls=%async_computation.12 | async-start | bytes 262144 | tf_op jit(solution)/shard_map/all_to_all | solution.py:193
  227.2 13.0 %all-to-all-start.11 = ((f32[4,128,256]{2,1,0:T(8,128)}), f32[4,128,256]{2,1,0:T(8,128)S(1)}, u32[]{:S(2)}, u32[]{:S(2)}) async-start(f32[4,128,256]{2,1,0:T(8,128)} %broadcast_in_dim.10), calls=%async_computation.11 | async-start | bytes 1048576 | tf_op jit(solution)/shard_map/all_to_all | solution.py:237
  240.9 12.2 %all-to-all-start.13 = ((f32[16,16,256]{2,1,0:T(8,128)}), f32[16,16,256]{2,1,0:T(8,128)S(1)}, u32[]{:S(2)}, u32[]{:S(2)}) async-start(f32[16,16,256]{2,1,0:T(8,128)} %broadcast_in_dim.11), calls=%async_computation.13 | async-start | bytes 524288 | tf_op jit(solution)/shard_map/all_to_all | solution.py:195
  244.5 17.6 %collective-permute-start.3 = (f32[512,256]{1,0:T(8,128)S(1)}, f32[512,256]{1,0:T(8,128)S(1)}, u32[]{:S(2)}, u32[]{:S(2)}) collective-permute-start(f32[512,256]{1,0:T(8,128)S(1)} %bitcast.44), channel_id=1, source_target_pairs={{0,1},{1,0},{2,3},{3,2},{4,5},{5,4},{6,7},{7,6},{8,9},{9,8},{10,11... | collective-permute-start | bytes 1572872 | tf_op jit(solution)/shard_map/ppermute | solution.py:240
  263.9 11.0 %all-to-all-start.14 = ((f32[16,1,256]{2,1,0:T(1,128)}), f32[16,1,256]{2,1,0:T(1,128)S(1)}, u32[]{:S(2)}, u32[]{:S(2)}) async-start(f32[16,1,256]{2,1,0:T(1,128)} %copy.10), calls=%async_computation.14 | async-start | bytes 32768 | tf_op jit(solution)/shard_map/all_to_all | solution.py:260
  275.0 1.1 copy-start.8
